TPU v7x, 32 devices: a whole 2x2x4 slice. The times are simulated.
32 devices in a mesh: wide: 8 (over y, x, core), narrow: 4 (over z).
Axes of the slice: x: 2, y: 2, z: 4, core: 2. Of those that a mesh axis runs over, the one named last changes fastest.
Arguments:
- volume: bfloat16 [64, 16, 32, 512], P(None, 'wide', 'narrow'), may hold values from -6 to 6
- out_grad: bfloat16 [64, 16, 32, 512], P(None, 'wide', 'narrow'), may hold values from -6 to 6
- plane_kernel: bfloat16 [9, 64, 64], replicated, may hold values from -0.25 to 0.25
- z_axis_kernel: bfloat16 [7, 64, 64], replicated, may hold values from -0.25 to 0.25
Outputs:
- volume_grad: bfloat16 [64, 16, 32, 512], P(None, 'wide', 'narrow')
- plane_kernel_grad: float32 [9, 64, 64], replicated
- z_axis_kernel_gradient: float32 [7, 64, 64], replicated
All inputs are finite; a program needn't handle non-finite values.
Results may differ from a plain program's by a relative error of at most 0.0061.
Values may be sent and summed in bfloat16 or wider, within the bound.
A program may use at most 192 MiB of HBM per device.

v0:
```python
import math

import jax
import jax.numpy as jnp
from jax import lax
from jax.sharding import PartitionSpec as P

Z_DILATION = 4


def with_halo(block, sides, width):
    for axis, dim in sides:
        count = lax.axis_size(axis)
        forward = [(i, i + 1) for i in range(count - 1)]
        backward = [(target, source) for source, target in forward]
        low = lax.ppermute(
            lax.slice_in_dim(block, block.shape[dim] - width, None, axis=dim), axis, forward
        )
        high = lax.ppermute(lax.slice_in_dim(block, 0, width, axis=dim), axis, backward)
        block = jnp.concatenate([low, block, high], axis=dim)
    return block


def silu_slope(values):
    sigmoid = jax.nn.sigmoid(values)
    return sigmoid * (1.0 + values * (1.0 - sigmoid))


def plane_stack(rimmed, rows, cols, flipped):
    padded = jnp.pad(rimmed, ((0, 0), (0, 0), (0, 0), (1, 1)))
    pieces = []
    for kernel_tap_index in range(9):
        source_tap = 8 - kernel_tap_index if flipped else kernel_tap_index
        row_shift = source_tap // 3
        col_shift = source_tap % 3
        pieces.append(padded[:, :, row_shift : row_shift + rows, col_shift : col_shift + cols])
    return jnp.concatenate(pieces, axis=0)


def depth_stack(pencil, kernel_extent, flipped):
    depth_axis_size = pencil.shape[1]
    padded = jnp.pad(pencil, ((0, 0), (kernel_extent, kernel_extent), (0, 0)))
    pieces = []
    for kernel_tap_index in range(7):
        source_tap = 6 - kernel_tap_index if flipped else kernel_tap_index
        start = source_tap * Z_DILATION
        pieces.append(padded[:, start : start + depth_axis_size])
    return jnp.concatenate(pieces, axis=0)


def stacked_mixing(weight, stacked, out_shape):
    mixed = jnp.dot(
        weight, stacked.reshape(stacked.shape[0], -1), preferred_element_type=jnp.float32
    )
    return mixed.reshape(out_shape)


def stacked_kernel_grad(left, stacked, taps):
    width = left.shape[0]
    product = jnp.dot(
        left.reshape(width, -1),
        stacked.reshape(stacked.shape[0], -1).T,
        preferred_element_type=jnp.float32,
    )
    return product.reshape(width, taps, width).transpose(1, 0, 2)


def on_device(volume, out_grad, plane_kernel, z_axis_kernel):
    width, slabs, rows, cols = volume.shape
    cells = rows * cols
    kernel_extent = 3 * Z_DILATION
    plane_forward = plane_kernel.transpose(1, 0, 2).reshape(width, 9 * width)
    plane_backward = plane_kernel.transpose(2, 0, 1).reshape(width, 9 * width)
    depth_forward = z_axis_kernel.transpose(1, 0, 2).reshape(width, 7 * width)
    depth_backward = z_axis_kernel.transpose(2, 0, 1).reshape(width, 7 * width)
    rimmed = with_halo(volume, (("narrow", 2),), 1)
    volume_stack = plane_stack(rimmed, rows, cols, False)
    pre_act = stacked_mixing(plane_forward, volume_stack, volume.shape)
    acts = jax.nn.silu(pre_act).astype(jnp.bfloat16)
    act_slab = acts.reshape(width, slabs, cells)
    act_pencil, grad_pencil = (
        lax.all_to_all(act_slab, "wide", split_axis=2, concat_axis=1, tiled=True),
        lax.all_to_all(
            out_grad.reshape(width, slabs, cells), "wide", split_axis=2, concat_axis=1, tiled=True
        ),
    )
    depth_axis_size = act_pencil.shape[1]
    act_stack = depth_stack(act_pencil, kernel_extent, False)
    depth_output = stacked_mixing(depth_forward, act_stack, act_pencil.shape)
    depth_gradient = (grad_pencil.astype(jnp.float32) * silu_slope(depth_output)).astype(
        jnp.bfloat16
    )
    depth_term = stacked_kernel_grad(depth_gradient, act_stack, 7)
    grad_stack = depth_stack(depth_gradient, kernel_extent, True)
    activation_gradient = stacked_mixing(depth_backward, grad_stack, act_pencil.shape).astype(
        jnp.bfloat16
    )
    slab_grad = lax.all_to_all(
        activation_gradient, "wide", split_axis=1, concat_axis=2, tiled=True
    ).reshape(width, slabs, rows, cols)
    gradient_scale = 1.0 / math.sqrt(depth_axis_size * rows * lax.axis_size("narrow") * cols)
    pre_grad = (slab_grad.astype(jnp.float32) * silu_slope(pre_act)).astype(jnp.bfloat16)
    plane_term = stacked_kernel_grad(pre_grad, volume_stack, 9)
    grad_rimmed = with_halo(pre_grad, (("narrow", 2),), 1)
    pre_stack = plane_stack(grad_rimmed, rows, cols, True)
    volume_grad = out_grad.astype(jnp.float32) + stacked_mixing(
        plane_backward, pre_stack, volume.shape
    )
    plane_total, depth_total = lax.psum((plane_term, depth_term), ("wide", "narrow"))
    return (
        volume_grad.astype(jnp.bfloat16),
        plane_total * gradient_scale,
        depth_total * gradient_scale,
    )


def solution(mesh):
    return jax.shard_map(
        on_device,
        mesh=mesh,
        in_specs=(P(None, "wide", "narrow", None), P(None, "wide", "narrow", None), P(), P()),
        out_specs=(P(None, "wide", "narrow", None), P(), P()),
        check_vma=False,
    )
```

profile of v0, /device:TPU:0, one launch (start us, length us, event | category | flops | bytes accessed | tf_op | source)
XLA Modules:
  0.0 398.0 jit_solution(4483052175532594992)
XLA Ops:
  7.2 2.0 fusion.60
  9.9 5.6 %collective-permute-start = (bf16[64,2,1,512]{3,0,2,1:T(8,128)(2,1)}, bf16[64,2,1,512]{3,0,2,1:T(8,128)(2,1)}, u32[]{:S(2)}, u32[]{:S(2)}) collective-permute-start(bf16[64,2,1,512]{3,0,2,1:T(8,128)(2,1)} %copy.137), channel_id=1, source_target_pairs={{0,1},{1,2},{2,3},{4,5},{5,6},{6,7},{8,9},{9,10},{10,11},{12,13},{... | collective-permute-start | bytes 393224 | tf_op jit(solution)/shard_map/ppermute | solution.py:16
  17.4 3.4 copy.108
  20.9 2.7 reshape.102
  23.5 4.3 %all-to-all-start = ((bf16[8,2,32768]{2,1,0:T(2,128)(2,1)}), bf16[8,2,32768]{2,1,0:T(2,128)(2,1)}, u32[]{:S(2)}, u32[]{:S(2)}) async-start(bf16[8,2,32768]{2,1,0:T(2,128)(2,1)} %reshape.102), calls=%async_computation | async-start | bytes 2097152 | tf_op jit(solution)/shard_map/all_to_all | solution.py:83
  30.2 3.5 fusion.6
  34.9 1.5 fusion.52
  36.4 1.5 slice_dynamic-update-slice_fusion.10
  40.2 1.9 slice_dynamic-update-slice_fusion.8
  43.4 1.6 fusion.51
  45.0 1.8 slice_dynamic-update-slice_fusion.6
  46.8 18.8 %copy.147 = bf16[72,8,16,512]{3,1,2,0:T(8,128)(2,1)} copy(bf16[72,8,16,512]{3,2,1,0:T(8,128)(2,1)} %bitcast.47) | data formatting | bytes 18874368
  65.6 5.6 %fusion.61 = f32[8192,64]{0,1:T(8,128)S(1)} fusion(bf16[576,8192]{1,0:T(8,128)(2,1)} %bitcast.170, bf16[64,576]{0,1:T(8,128)(2,1)S(1)} %bitcast.205), kind=kOutput, calls=%fused_computation.118 | convolution fusion | flops 603979776 | bytes 11608064 | tf_op jit(solution)/shard_map/dot_general | solution.py:52
  71.7 3.9 copy.119
  75.7 4.4 %reshape.104 = bf16[8,2,32768]{2,1,0:T(2,128)(2,1)} reshape(bf16[4096,2,64]{2,1,0:T(2,128)(2,1)} %bitcast.186) | data formatting | bytes 2097152
  80.0 4.1 %all-to-all-start.1 = ((bf16[8,2,32768]{2,1,0:T(2,128)(2,1)}), bf16[8,2,32768]{2,1,0:T(2,128)(2,1)S(1)}, u32[]{:S(2)}, u32[]{:S(2)}) async-start(bf16[8,2,32768]{2,1,0:T(2,128)(2,1)} %reshape.104), calls=%async_computation.1 | async-start | bytes 2097152 | tf_op jit(solution)/shard_map/all_to_all | solution.py:82
  85.0 4.3 %reshape.103 = bf16[4096,2,64]{2,1,0:T(2,128)(2,1)} reshape(bf16[8,2,32768]{2,1,0:T(2,128)(2,1)} %all-to-all-done) | data formatting | bytes 2097152
  89.3 6.3 %copy.109 = f32[64,2,8,512]{3,1,2,0:T(2,128)} copy(bf16[64,2,8,512]{0,1,3,2:T(2,128)(2,1)} %bitcast.189) | data formatting | bytes 3145728 | tf_op jit(solution)/shard_map/convert_element_type | solution.py:90
  95.6 3.7 reshape.93
  99.5 2.7 reshape.105
  102.2 4.6 %copy.136 = bf16[64,2,8,512]{3,0,1,2:T(8,128)(2,1)S(1)} copy(bf16[64,2,8,512]{0,1,3,2:T(2,128)(2,1)} %bitcast.177) | data formatting | bytes 2097152 | tf_op jit(solution)/shard_map/all_to_all | solution.py:82
  106.8 4.3 %copy.135 = bf16[64,2,8,512]{3,2,0,1:T(8,128)(2,1)} copy(bf16[64,2,8,512]{0,1,3,2:T(2,128)(2,1)} %bitcast.178) | data formatting | bytes 2097152 | tf_op jit(solution)/shard_map/all_to_all | solution.py:82
  111.2 2.0 fusion.42
  116.5 2.1 copy.125
  118.6 2.8 concatenate.52
  121.5 1.4 copy.144
  130.6 4.5 %fusion.63 = f32[8192,64]{0,1:T(8,128)S(1)} fusion(bf16[64,448]{1,0:T(8,128)(2,1)S(1)} %copy-done.16, bf16[448,8192]{1,0:T(8,128)(2,1)} %constant_dynamic-update-slice_fusion.1), kind=kOutput, calls=%fused_computation.120 | convolution fusion | flops 469762048 | bytes 9494528 | tf_op jit(solution)/shard_map/dot_general | solution.py:52
  139.9 2.9 copy-done.1
  142.8 11.6 %copy.149 = bf16[56,8,16,512]{3,1,2,0:T(8,128)(2,1)S(1)} copy(bf16[56,8,16,512]{3,2,1,0:T(8,128)(2,1)} %bitcast.182) | data formatting | bytes 14680064
  154.4 1.5 convolution_convert_fusion
  157.0 3.9 all-to-all-start.2
  160.9 15.4 %dot_general.35 = bf16[9,64,8192]{2,1,0:T(8,128)(2,1)} reshape(bf16[576,2,8,512]{3,2,1,0:T(8,128)(2,1)} %slice_dynamic-update-slice_fusion.6) | data formatting | bytes 18874368 | tf_op jit(solution)/shard_map/dot_general | solution.py:60
  176.3 2.5 copy.150
  178.8 4.0 %reshape.95 = f32[64,8192]{1,0:T(8,128)} reshape(f32[64,8,2,512]{3,2,1,0:T(2,128)} %bitcast.180) | data formatting | bytes 4194304 | tf_op jit(solution)/shard_map/convert_element_type | solution.py:90
  182.9 8.4 %convolution_bitcast_fusion.1 = f32[7,64,64]{2,1,0:T(8,128)} fusion(bf16[7,64,8192]{2,1,0:T(8,128)(2,1)} %bitcast.174, f32[64,8192]{1,0:T(8,128)} %reshape.95, f32[8192,64]{0,1:T(8,128)} %copy-done.4), kind=kOutput, calls=%fused_computation.66 | convolution fusion | flops 474480640 | bytes 11649024 | tf_op jit(solution)/shard_map/dot_general | solution.py:60
  194.6 1.6 multiply_convert_fusion
  196.3 8.8 %convolution_bitcast_fusion = f32[9,64,64]{2,1,0:T(8,128)} fusion(bf16[9,64,8192]{2,1,0:T(8,128)(2,1)} %dot_general.35, f32[64,8192]{1,0:T(8,128)S(1)} %bitcast.202, f32[8192,64]{0,1:T(8,128)S(1)} %fusion.61), kind=kOutput, calls=%fused_computation.65 | convolution fusion | flops 608698368 | bytes 13778944 | tf_op jit(solution)/shard_map/dot_general | solution.py:60
  205.1 4.6 %collective-permute-start.2 = (bf16[64,2,1,512]{3,0,1,2:T(8,128)(2,1)S(1)}, bf16[64,2,1,512]{3,0,1,2:T(8,128)(2,1)S(1)}, u32[]{:S(2)}, u32[]{:S(2)}) collective-permute-start(bf16[64,2,1,512]{3,0,1,2:T(8,128)(2,1)S(1)} %get-tuple-element.5), channel_id=1, source_target_pairs={{0,1},{1,2},{2,3},{4,5},{5,6},{6,7},{8,9},{9,10},{10,11},{12,13},{... | collective-permute-start | bytes 393224 | tf_op jit(solution)/shard_map/ppermute | solution.py:16
  209.7 1.5 collective-permute-start.3
  211.2 125.0 %all-reduce.7.cloned.1.call-done = (f32[9,64,64]{2,1,0:T(8,128)}, f32[7,64,64]{2,1,0:T(8,128)}) async-done(((f32[9,64,64]{2,1,0:T(8,128)}, f32[7,64,64]{2,1,0:T(8,128)}), (f32[9,64,64]{2,1,0:T(8,128)}, f32[7,64,64]{2,1,0:T(8,128)})) %all-reduce.7.cloned.1.call-update) | async-done | bytes 262160 | tf_op jit(solution)/shard_map/psum | solution.py:109
  336.2 1.7 broadcast_multiply_fusion
  337.9 1.6 broadcast_multiply_fusion.1
  340.4 1.5 slice_dynamic-update-slice_fusion.5
  344.2 1.5 slice_dynamic-update-slice_fusion.3
  347.9 1.5 slice_dynamic-update-slice_fusion.1
  351.5 12.7 %copy.133 = bf16[576,2,8,512]{3,2,1,0:T(8,128)(2,1)} copy(bf16[576,2,8,512]{3,0,1,2:T(8,128)(2,1)} %slice_dynamic-update-slice_fusion) | data formatting | bytes 18874368 | tf_op jit(solution)/shard_map/concatenate | solution.py:37
  364.2 18.5 %copy.151 = bf16[72,8,16,512]{3,1,2,0:T(8,128)(2,1)} copy(bf16[72,8,16,512]{3,2,1,0:T(8,128)(2,1)} %bitcast.173) | data formatting | bytes 18874368
  382.7 5.6 %fusion.62 = f32[8192,64]{0,1:T(8,128)S(1)} fusion(bf16[576,8192]{1,0:T(8,128)(2,1)} %bitcast.171, bf16[64,576]{0,1:T(8,128)(2,1)S(1)} %bitcast.204), kind=kOutput, calls=%fused_computation.119 | convolution fusion | flops 603979776 | bytes 11608064 | tf_op jit(solution)/shard_map/dot_general | solution.py:52
  (90 shorter events, 41.9 us)
Async XLA Ops:
  9.9 18.1 %collective-permute-start = (bf16[64,2,1,512]{3,0,2,1:T(8,128)(2,1)}, bf16[64,2,1,512]{3,0,2,1:T(8,128)(2,1)}, u32[]{:S(2)}, u32[]{:S(2)}) collective-permute-start(bf16[64,2,1,512]{3,0,2,1:T(8,128)(2,1)} %copy.137), channel_id=1, source_target_pairs={{0,1},{1,2},{2,3},{4,5},{5,6},{6,7},{8,9},{9,10},{10,11},{12,13},{... | collective-permute-start | bytes 393224 | tf_op jit(solution)/shard_map/ppermute | solution.py:16
  16.2 12.9 %collective-permute-start.1 = (bf16[64,2,1,512]{3,0,2,1:T(8,128)(2,1)}, bf16[64,2,1,512]{3,0,2,1:T(8,128)(2,1)}, u32[]{:S(2)}, u32[]{:S(2)}) collective-permute-start(bf16[64,2,1,512]{3,0,2,1:T(8,128)(2,1)} %copy.138), channel_id=1, source_target_pairs={{1,0},{2,1},{3,2},{5,4},{6,5},{7,6},{9,8},{10,9},{11,10},{13,12},{... | collective-permute-start | bytes 393224 | tf_op jit(solution)/shard_map/ppermute | solution.py:19
  20.9 7.0 %copy-start.14 = (bf16[9,64,64]{2,1,0:T(8,128)(2,1)S(1)}, bf16[9,64,64]{2,1,0:T(8,128)(2,1)}, u32[]{:S(2)}) copy-start(bf16[9,64,64]{2,1,0:T(8,128)(2,1)} %param.6) | copy-start | bytes 221188
  20.9 9.4 %copy-start = (bf16[64,2,8,512]{3,2,1,0:T(8,128)(2,1)S(1)}, bf16[64,2,8,512]{3,2,1,0:T(8,128)(2,1)}, u32[]{:S(2)}) copy-start(bf16[64,2,8,512]{3,2,1,0:T(8,128)(2,1)} %param.4) | copy-start | bytes 3145732
  23.5 56.5 %all-to-all-start = ((bf16[8,2,32768]{2,1,0:T(2,128)(2,1)}), bf16[8,2,32768]{2,1,0:T(2,128)(2,1)}, u32[]{:S(2)}, u32[]{:S(2)}) async-start(bf16[8,2,32768]{2,1,0:T(2,128)(2,1)} %reshape.102), calls=%async_computation | async-start | bytes 2097152 | tf_op jit(solution)/shard_map/all_to_all | solution.py:83
  75.7 8.5 %copy-start.15 = (bf16[7,64,64]{2,1,0:T(8,128)(2,1)S(1)}, bf16[7,64,64]{2,1,0:T(8,128)(2,1)}, u32[]{:S(2)}) copy-start(bf16[7,64,64]{2,1,0:T(8,128)(2,1)} %param.7) | copy-start | bytes 172036
  80.0 19.5 %all-to-all-start.1 = ((bf16[8,2,32768]{2,1,0:T(2,128)(2,1)}), bf16[8,2,32768]{2,1,0:T(2,128)(2,1)S(1)}, u32[]{:S(2)}, u32[]{:S(2)}) async-start(bf16[8,2,32768]{2,1,0:T(2,128)(2,1)} %reshape.104), calls=%async_computation.1 | async-start | bytes 2097152 | tf_op jit(solution)/shard_map/all_to_all | solution.py:82
  114.3 2.2 copy-start.8
  118.6 4.3 %copy-start.9 = (bf16[16,8,8,512]{3,2,1,0:T(8,128)(2,1)S(1)}, bf16[16,8,8,512]{3,2,1,0:T(8,128)(2,1)}, u32[]{:S(2)}) copy-start(bf16[16,8,8,512]{3,2,1,0:T(8,128)(2,1)} %get-tuple-element.11) | copy-start | bytes 3145732
  121.5 1.6 copy-start.7
  122.9 1.3 copy-start.11
  123.0 2.2 copy-start.12
  123.1 3.2 copy-start.13
  128.4 2.2 copy-start.16
  135.1 1.4 copy-start.4
  135.1 2.6 copy-start.5
  139.9 2.9 copy-start.1
  157.0 34.3 %all-to-all-start.2 = ((bf16[64,16,512]{2,0,1:T(8,128)(2,1)}), bf16[64,16,512]{2,0,1:T(8,128)(2,1)S(1)}, u32[]{:S(2)}, u32[]{:S(2)}) async-start(bf16[64,16,512]{2,0,1:T(8,128)(2,1)} %bitcast.197), calls=%async_computation.2 | async-start | bytes 2097152 | tf_op jit(solution)/shard_map/all_to_all | solution.py:98
  160.9 175.3 %all-reduce.7.cloned.1.call-start = ((), (), s32[]{:S(2)}) async-start(), calls=%async_computation.3 | async-start | bytes 1048576 | tf_op jit(solution)/shard_map/psum | solution.py:109
  191.3 1.5 copy-start.2
  192.8 1.6 copy-start.6
  192.8 1.8 copy-start.3
  205.1 134.4 %collective-permute-start.2 = (bf16[64,2,1,512]{3,0,1,2:T(8,128)(2,1)S(1)}, bf16[64,2,1,512]{3,0,1,2:T(8,128)(2,1)S(1)}, u32[]{:S(2)}, u32[]{:S(2)}) collective-permute-start(bf16[64,2,1,512]{3,0,1,2:T(8,128)(2,1)S(1)} %get-tuple-element.5), channel_id=1, source_target_pairs={{0,1},{1,2},{2,3},{4,5},{5,6},{6,7},{8,9},{9,10},{10,11},{12,13},{... | collective-permute-start | bytes 393224 | tf_op jit(solution)/shard_map/ppermute | solution.py:16
  209.7 129.8 %collective-permute-start.3 = (bf16[64,2,1,512]{3,0,1,2:T(8,128)(2,1)S(1)}, bf16[64,2,1,512]{3,0,1,2:T(8,128)(2,1)S(1)}, u32[]{:S(2)}, u32[]{:S(2)}) collective-permute-start(bf16[64,2,1,512]{3,0,1,2:T(8,128)(2,1)S(1)} %get-tuple-element.6), channel_id=1, source_target_pairs={{1,0},{2,1},{3,2},{5,4},{6,5},{7,6},{9,8},{10,9},{11,10},{13,12},{... | collective-permute-start | bytes 393224 | tf_op jit(solution)/shard_map/ppermute | solution.py:19
  388.3 1.2 copy-start.10
Sparse Core Ops, SparseCore 0:
  205.2 130.9 all-reduce.6
where the time goes:
time: 403 us; the launch traced here: 398 us
  local copies, waits for them, and re-layouts  181 us (45%)
  waiting for transfers between devices  125 us (31%)
  matrix products  34.3 us (9%)
  starting transfers between devices  25.2 us (6%)
  other arithmetic  17.6 us (4%)
  between operations  14.7 us (4%)
    psum x1, waiting for transfers between devices, on_device(): lax.psum((plane_term, depth_term), ('wide', 'narrow'))  125 us
    unnamed x73, local copies, waits for them, and re-layouts  105 us
    dot_general x2, matrix products, stacked_kernel_grad(): jnp.dot(left.reshape(width, -1), stacked.reshape(stacked.shape[0], -1).T,...  17.2 us
    dot_general x4, matrix products, stacked_mixing(): jnp.dot(weight, stacked.reshape(stacked.shape[0], -1), preferred_element_...  17.1 us
    concatenate x3, local copies, waits for them, and re-layouts, plane_stack(): return jnp.concatenate(pieces, axis=0)  15.6 us
    dot_general x1, local copies, waits for them, and re-layouts, stacked_kernel_grad(): jnp.dot(left.reshape(width, -1), stacked.reshape(stacked.shape[0], -1).T,...  15.4 us
    convert_element_type x3, local copies, waits for them, and re-layouts, on_device(): grad_pencil.astype(jnp.float32) * silu_slope(depth_output)  14 us
    all_to_all x3, local copies, waits for them, and re-layouts, on_device(): lax.all_to_all(act_slab, 'wide', split_axis=2, concat_axis=1, tiled=True)  11.1 us
  transfers between devices with their start and end apart: 8, of which 2 were waited for; matrix products, arithmetic and copies ran while one was open for 27% of the time, Pallas kernels for 0%

commit v1 on v0

--- a/solution.py
+++ b/solution.py
@@ -1,8 +1,11 @@
+import functools
 import math
 
 import jax
 import jax.numpy as jnp
 from jax import lax
+from jax.experimental import pallas as pl
+from jax.experimental.pallas import tpu as pltpu
 from jax.sharding import PartitionSpec as P
 
 Z_DILATION = 4
@@ -114,9 +117,414 @@
     )
 
 
+BF16 = jnp.bfloat16
+F32 = jnp.float32
+MESH = pl.DeviceIdType.MESH
+TILES = 12
+
+
+def sigmoid_of(values):
+    return 0.5 * jnp.tanh(0.5 * values) + 0.5
+
+
+def shifted_stack(row):
+    wide_row = row.astype(F32)
+    cols = row.shape[1]
+    column = lax.broadcasted_iota(jnp.int32, row.shape, 1)
+    left = jnp.where(column == 0, 0.0, pltpu.roll(wide_row, 1, 1))
+    right = jnp.where(column == cols - 1, 0.0, pltpu.roll(wide_row, cols - 1, 1))
+    return jnp.concatenate([left.astype(BF16), row.astype(BF16), right.astype(BF16)], axis=0)
+
+
+def dot_nn(left, right):
+    return jnp.dot(left, right, preferred_element_type=F32)
+
+
+def dot_nt(left, right):
+    return lax.dot_general(left, right, (((1,), (1,)), ((), ())), preferred_element_type=F32)
+
+
+def block_kernel(
+    n, m, rows, scale,
+    vol, og, wf, wb, bigw, bigw_t,
+    vg, gsum,
+    volh, stack, slope, acts_out, acts_in, og_in, dg, ag_out, ag_in, pg_halo, plane_acc, depth_acc,
+    red_src, red_in, part, part_in, tot, tot_in,
+    vh_s, vh_r, og_s, og_r, ac_s, ac_r, ag_s, ag_r, ph_s, ph_r, r1_s, r1_r, r2_s, r2_r, r3_s, r3_r,
+):
+    me = lax.axis_index("wide")
+    mine = lax.axis_index("narrow")
+    ch = vol.shape[2]
+    cols = vol.shape[3]
+
+    def rcopy(source, target, send, recv, **where):
+        return pltpu.make_async_remote_copy(
+            src_ref=source, dst_ref=target, send_sem=send, recv_sem=recv,
+            device_id=where, device_id_type=MESH,
+        )
+
+    def wide_peer(step):
+        return lax.rem(me + step, n)
+
+    def narrow_peer(step):
+        return lax.rem(mine + step, m)
+
+    barrier = pltpu.get_barrier_semaphore()
+
+    @pl.loop(1, n)
+    def _(step):
+        pl.semaphore_signal(barrier, inc=1, device_id={"wide": wide_peer(step)}, device_id_type=MESH)
+
+    @pl.loop(1, m)
+    def _(step):
+        pl.semaphore_signal(barrier, inc=1, device_id={"narrow": narrow_peer(step)}, device_id_type=MESH)
+
+    pl.semaphore_wait(barrier, n + m - 2)
+
+    has_low = mine > 0
+    has_high = mine < m - 1
+    up = jnp.minimum(mine + 1, m - 1)
+    down = jnp.maximum(mine - 1, 0)
+
+    def vol_up():
+        return rcopy(vol.at[rows - 1], volh.at[0], vh_s.at[0], vh_r.at[0], narrow=up)
+
+    def vol_down():
+        return rcopy(vol.at[0], volh.at[rows + 1], vh_s.at[1], vh_r.at[1], narrow=down)
+
+    def og_copy(step):
+        peer = wide_peer(step)
+        return rcopy(og.at[peer], og_in.at[me // 2, lax.rem(me, 2)], og_s.at[peer], og_r.at[me], wide=peer)
+
+    def og_arrival(step):
+        peer = wide_peer(step)
+        return rcopy(og.at[peer], og_in.at[peer // 2, lax.rem(peer, 2)], og_s.at[peer], og_r.at[peer], wide=peer)
+
+    def act_copy(peer):
+        return rcopy(acts_out.at[peer], acts_in.at[me // 2, lax.rem(me, 2)], ac_s.at[peer], ac_r.at[me], wide=peer)
+
+    def act_arrival(peer):
+        return rcopy(acts_out.at[peer], acts_in.at[peer // 2, lax.rem(peer, 2)], ac_s.at[peer], ac_r.at[peer], wide=peer)
+
+    def ag_copy(peer):
+        return rcopy(ag_out.at[peer // 2, lax.rem(peer, 2)], ag_in.at[me], ag_s.at[peer], ag_r.at[me], wide=peer)
+
+    def ag_arrival(peer):
+        return rcopy(ag_out.at[peer // 2, lax.rem(peer, 2)], ag_in.at[peer], ag_s.at[peer], ag_r.at[peer], wide=peer)
+
+    def pg_up():
+        return rcopy(stack.at[rows, :, pl.ds(ch, ch)], pg_halo.at[0], ph_s.at[0], ph_r.at[0], narrow=up)
+
+    def pg_down():
+        return rcopy(stack.at[1, :, pl.ds(ch, ch)], pg_halo.at[1], ph_s.at[1], ph_r.at[1], narrow=down)
+
+    def r1_copy(peer):
+        return rcopy(red_src.at[peer], red_in.at[me], r1_s.at[peer], r1_r.at[me], wide=peer)
+
+    def r1_arrival(peer):
+        return rcopy(red_src.at[peer], red_in.at[peer], r1_s.at[peer], r1_r.at[peer], wide=peer)
+
+    def r2_copy(peer):
+        return rcopy(part, part_in.at[mine], r2_s.at[peer], r2_r.at[mine], narrow=peer)
+
+    def r2_arrival(peer):
+        return rcopy(part, part_in.at[peer], r2_s.at[peer], r2_r.at[peer], narrow=peer)
+
+    def r3_copy(peer):
+        return rcopy(tot, tot_in.at[me], r3_s.at[peer], r3_r.at[me], wide=peer)
+
+    def r3_arrival(peer):
+        return rcopy(tot, tot_in.at[peer], r3_s.at[peer], r3_r.at[peer], wide=peer)
+
+    @pl.when(has_high)
+    def _():
+        vol_up().start()
+
+    @pl.when(has_low)
+    def _():
+        vol_down().start()
+
+    @pl.loop(1, n)
+    def _(step):
+        og_copy(step).start()
+
+    og_in[me // 2, lax.rem(me, 2)] = og[me]
+
+    @pl.when(jnp.logical_not(has_low))
+    def _():
+        volh[0] = jnp.zeros(volh.shape[1:], BF16)
+
+    @pl.when(jnp.logical_not(has_high))
+    def _():
+        volh[rows + 1] = jnp.zeros(volh.shape[1:], BF16)
+
+    @pl.loop(0, rows)
+    def _(x):
+        for z in range(2):
+            row = vol[x, z]
+            volh[x + 1, z] = row
+            stack[x + 1, z] = shifted_stack(row)
+
+    @pl.when(has_high)
+    def _():
+        vol_up().wait_send()
+        vol_down().wait_recv()
+
+    @pl.when(has_low)
+    def _():
+        vol_down().wait_send()
+        vol_up().wait_recv()
+
+    for x in (0, rows + 1):
+        for z in range(2):
+            stack[x, z] = shifted_stack(volh[x, z])
+
+    @pl.loop(1, n + 1)
+    def _(step):
+        x = wide_peer(step)
+        for z in range(2):
+            v = dot_nn(wf[...], stack[pl.ds(x, 3), z].reshape(9 * ch, cols))
+            g = sigmoid_of(v)
+            acts_out[x, z] = (v * g).astype(BF16)
+            slope[x, z] = g * (1.0 + v * (1.0 - g))
+
+        @pl.when(step < n)
+        def _():
+            act_copy(x).start()
+
+    acts_in[me // 2, lax.rem(me, 2)] = acts_out[me]
+
+    @pl.loop(1, n)
+    def _(step):
+        og_arrival(step).wait_recv()
+        act_arrival(wide_peer(step)).wait_recv()
+
+    @pl.loop(0, 2)
+    def _(half):
+        for b in range(2):
+            pencil = acts_in[:, half, b].reshape(4 * ch, cols)
+            v = dot_nn(bigw[...], pencil)
+            g = sigmoid_of(v)
+            cot = og_in[:, half, b].reshape(4 * ch, cols).astype(F32)
+            grad = (cot * (g * (1.0 + v * (1.0 - g)))).astype(BF16)
+            dg[half, b] = grad
+            back = dot_nn(bigw_t[...], grad).astype(BF16)
+            ag_out[:, half, b] = back.reshape(4, ch, cols)
+        for q in range(4):
+            peer = 2 * q + half
+
+            @pl.when(peer != me)
+            def _():
+                ag_copy(peer).start()
+
+            @pl.when(peer == me)
+            def _():
+                ag_in[me] = ag_out[q, half]
+
+    depth_acc[...] = jnp.zeros_like(depth_acc)
+    plane_acc[...] = jnp.zeros_like(plane_acc)
+
+    @pl.loop(0, 2)
+    def _(half):
+        for b in range(2):
+            depth_acc[...] += dot_nt(dg[half, b], acts_in[:, half, b].reshape(4 * ch, cols))
+
+    for d in range(-3, 3):
+        tile = jnp.zeros((ch, 128), F32)
+        for q in range(4):
+            for t in range(2):
+                if 2 * t - q == d:
+                    tile = tile + depth_acc[q * ch : (q + 1) * ch, 128 * t : 128 * (t + 1)]
+        red_src[:, d + 3] = tile.reshape(n, ch // n, 128)
+
+    @pl.loop(0, rows)
+    def _(step):
+        x = lax.rem(step + rows - 1, rows)
+
+        @pl.when(x != me)
+        def _():
+            ag_arrival(x).wait_recv()
+
+        for z in range(2):
+            row = ag_in[x, z].astype(F32) * slope[x, z]
+            shifted = shifted_stack(row.astype(BF16))
+            stack[x + 1, z] = shifted
+            plane_acc[...] += dot_nt(shifted, volh[pl.ds(x, 3), z].reshape(3 * ch, cols))
+
+        @pl.when(step == 1)
+        def _():
+            @pl.when(has_high)
+            def _():
+                pg_up().start()
+
+            @pl.when(has_low)
+            def _():
+                pg_down().start()
+
+    for s in range(3):
+        red_src[:, 6 + 2 * s] = plane_acc[s * ch : (s + 1) * ch, 0:128].reshape(n, ch // n, 128)
+        rest = jnp.concatenate(
+            [plane_acc[s * ch : (s + 1) * ch, 128:192], jnp.zeros((ch, 64), F32)], axis=1
+        )
+        red_src[:, 7 + 2 * s] = rest.reshape(n, ch // n, 128)
+
+    @pl.loop(1, n)
+    def _(step):
+        r1_copy(wide_peer(step)).start()
+
+    red_in[me] = red_src[me]
+
+    def volume_rows(low, high):
+        @pl.loop(low, high)
+        def _(x):
+            for z in range(2):
+                out = dot_nn(wb[...], stack[pl.ds(x, 3), z].reshape(9 * ch, cols))
+                vg[x, z] = (og[x, z].astype(F32) + out).astype(BF16)
+
+    volume_rows(1, 3)
+
+    @pl.loop(1, n)
+    def _(step):
+        r1_arrival(wide_peer(step)).wait_recv()
+
+    part[...] = jnp.sum(red_in[...], axis=0)
+
+    @pl.loop(1, m)
+    def _(step):
+        r2_copy(narrow_peer(step)).start()
+
+    part_in[mine] = part[...]
+    volume_rows(3, 5)
+
+    @pl.loop(1, m)
+    def _(step):
+        r2_arrival(narrow_peer(step)).wait_recv()
+
+    tot[...] = jnp.sum(part_in[...], axis=0) * scale
+
+    @pl.loop(1, n)
+    def _(step):
+        r3_copy(wide_peer(step)).start()
+
+    tot_in[me] = tot[...]
+    volume_rows(5, rows - 1)
+
+    @pl.when(has_high)
+    def _():
+        pg_up().wait_send()
+        pg_down().wait_recv()
+
+    @pl.when(has_low)
+    def _():
+        pg_down().wait_send()
+        pg_up().wait_recv()
+
+    @pl.when(has_low)
+    def _():
+        for z in range(2):
+            stack[0, z] = shifted_stack(pg_halo[0, z])
+
+    @pl.when(has_high)
+    def _():
+        for z in range(2):
+            stack[rows + 1, z] = shifted_stack(pg_halo[1, z])
+
+    @pl.when(jnp.logical_not(has_low))
+    def _():
+        stack[0] = jnp.zeros(stack.shape[1:], BF16)
+
+    @pl.when(jnp.logical_not(has_high))
+    def _():
+        stack[rows + 1] = jnp.zeros(stack.shape[1:], BF16)
+
+    volume_rows(0, 1)
+    volume_rows(rows - 1, rows)
+
+    @pl.loop(1, n)
+    def _(step):
+        peer = wide_peer(step)
+        r3_arrival(peer).wait_recv()
+        og_copy(step).wait_send()
+        act_copy(peer).wait_send()
+        ag_copy(peer).wait_send()
+        r1_copy(peer).wait_send()
+        r3_copy(peer).wait_send()
+
+    @pl.loop(1, m)
+    def _(step):
+        r2_copy(narrow_peer(step)).wait_send()
+
+    gsum[...] = tot_in[...]
+
+
+def fused_block(n, m, volume, out_grad, plane_kernel, z_axis_kernel):
+    ch, _, rows, cols = volume.shape
+    vol = volume.transpose(2, 1, 0, 3)
+    og = out_grad.transpose(2, 1, 0, 3)
+    wf = plane_kernel.transpose(1, 0, 2).reshape(ch, 9 * ch)
+    wb = plane_kernel[::-1].transpose(2, 0, 1).reshape(ch, 9 * ch)
+    bigw = jnp.concatenate(
+        [z_axis_kernel[3 - q : 7 - q].transpose(1, 0, 2).reshape(ch, 4 * ch) for q in range(4)], axis=0
+    )
+    scale = 1.0 / math.sqrt(2 * n * rows * m * cols)
+    own = (rows, 2, ch, cols)
+    pencil = (4, 2, 2, ch, cols)
+    piece = (TILES, ch // n, 128)
+    sems = []
+    for count in (2, n, n, n, 2, n, m, n):
+        sems += [pltpu.SemaphoreType.DMA((count,))] * 2
+    vmem = pl.BlockSpec(memory_space=pltpu.VMEM)
+    vg, gsum = pl.pallas_call(
+        functools.partial(block_kernel, n, m, rows, scale),
+        out_shape=(jax.ShapeDtypeStruct(own, BF16), jax.ShapeDtypeStruct((n,) + piece, F32)),
+        in_specs=[vmem] * 6,
+        out_specs=(vmem, vmem),
+        scratch_shapes=[
+            pltpu.VMEM((rows + 2, 2, ch, cols), BF16),
+            pltpu.VMEM((rows + 2, 2, 3 * ch, cols), BF16),
+            pltpu.VMEM(own, F32),
+            pltpu.VMEM(own, BF16),
+            pltpu.VMEM(pencil, BF16),
+            pltpu.VMEM(pencil, BF16),
+            pltpu.VMEM((2, 2, 4 * ch, cols), BF16),
+            pltpu.VMEM(pencil, BF16),
+            pltpu.VMEM((n, 2, ch, cols), BF16),
+            pltpu.VMEM((2, 2, ch, cols), BF16),
+            pltpu.VMEM((3 * ch, 3 * ch), F32),
+            pltpu.VMEM((4 * ch, 4 * ch), F32),
+            pltpu.VMEM((n,) + piece, F32),
+            pltpu.VMEM((n,) + piece, F32),
+            pltpu.VMEM(piece, F32),
+            pltpu.VMEM((m,) + piece, F32),
+            pltpu.VMEM(piece, F32),
+            pltpu.VMEM((n,) + piece, F32),
+        ]
+        + sems,
+        compiler_params=pltpu.CompilerParams(
+            collective_id=0, has_side_effects=True, vmem_limit_bytes=52 * 1024 * 1024
+        ),
+    )(vol, og, wf, wb, bigw, bigw.T)
+    tiles = gsum.transpose(1, 0, 2, 3).reshape(TILES, ch, 2, ch)
+    low = tiles[:6, :, 0]
+    high = tiles[:6, :, 1]
+    edge = jnp.zeros((1, ch, ch), F32)
+    depth = jnp.concatenate([low, edge]) + jnp.concatenate([edge, high])
+    plane = tiles[6:].reshape(3, 2, ch, 2, ch)[::-1].transpose(1, 3, 0, 2, 4)
+    plane = plane.reshape(4, 3, ch, ch)[:3].reshape(9, ch, ch)
+    return vg.transpose(2, 1, 0, 3), plane, depth
+
+
 def solution(mesh):
+    n, m = mesh.shape["wide"], mesh.shape["narrow"]
+
+    def body(volume, out_grad, plane_kernel, z_axis_kernel):
+        ch, slabs, rows, cols = volume.shape
+        if n == 8 and slabs == 2 and rows == n and ch == 64 and m > 1:
+            return fused_block(n, m, volume, out_grad, plane_kernel, z_axis_kernel)
+        return on_device(volume, out_grad, plane_kernel, z_axis_kernel)
+
     return jax.shard_map(
-        on_device,
+        body,
         mesh=mesh,
         in_specs=(P(None, "wide", "narrow", None), P(None, "wide", "narrow", None), P(), P()),
         out_specs=(P(None, "wide", "narrow", None), P(), P()),

time: 403 us -> 74.3 us (0.18); the launches traced: 398 us -> 74 us
  local copies, waits for them, and re-layouts: 181 us -> 10 us
  waiting for transfers between devices: 125 us -> 0 us
  Pallas kernels: 0 us -> 62.3 us
  matrix products: 34.3 us -> 0 us
  starting transfers between devices: 25.2 us -> 0 us
  other arithmetic: 17.6 us -> 0.97 us
  between operations: 14.7 us -> 0.77 us
    psum x1 -> x0, waiting for transfers between devices: 125 us -> none  [on_device(): lax.psum((plane_term, depth_term), ('wide', 'narrow'))]
    unnamed x73 -> x9, local copies, waits for them, and re-layouts: 105 us -> 3.76 us
    pallas_call x0 -> x1, Pallas kernels: none -> 62.3 us  [fused_block(): pl.pallas_call(functools.partial(block_kernel, n, m, rows, scale), out_sh...]
    dot_general x6 -> x0, matrix products: 34.3 us -> none  [the longest x2 17.2 us: stacked_kernel_grad(): jnp.dot(left.reshape(width, -1), stacked.reshape(stacked.shape[0], -1).T,...]
    concatenate x12 -> x1, local copies, waits for them, and re-layouts: 23.5 us -> 0.1 us  [fused_block(): jnp.concatenate([z_axis_kernel[3 - q:7 - q].transpose(1, 0, 2).reshape(ch...]
    convert_element_type x6 -> x0, local copies, waits for them, and re-layouts: 20.2 us -> none  [the longest x3 14 us: on_device(): grad_pencil.astype(jnp.float32) * silu_slope(depth_output)]
    dot_general x1 -> x0, local copies, waits for them, and re-layouts: 15.4 us -> none  [stacked_kernel_grad(): jnp.dot(left.reshape(width, -1), stacked.reshape(stacked.shape[0], -1).T,...]
    ppermute x4 -> x0, starting transfers between devices: 12.9 us -> none  [the longest x2 10.1 us: with_halo(): lax.ppermute(lax.slice_in_dim(block, block.shape[dim] - width, None, axis...]
  transfers between devices with their start and end apart: 8 -> 0, of which waited for: 2 -> 0; matrix products, arithmetic and copies ran while one was open for 27% -> 0% of each run, Pallas kernels for 0% -> 0%
where the time goes in v1:
time: 74.3 us; the launch traced here: 74 us
  Pallas kernels  62.3 us (84%)
  local copies, waits for them, and re-layouts  10 us (13%)
  other arithmetic  0.97 us (1%)
  between operations  0.77 us (1%)
    pallas_call x1, Pallas kernels, fused_block(): pl.pallas_call(functools.partial(block_kernel, n, m, rows, scale), out_sh...  62.3 us
    unnamed x9, local copies, waits for them, and re-layouts  3.76 us
    transpose x1, local copies, waits for them, and re-layouts, fused_block(): og = out_grad.transpose(2, 1, 0, 3)  2.47 us

profile of v1, /device:TPU:0, one launch (start us, length us, event | category | flops | bytes accessed | tf_op | source)
XLA Modules:
  0.0 74.0 jit_solution(12249889385709645686)
XLA Ops:
  0.6 1.0 %copy.33 = bf16[64,9,64]{0,2,1:T(8,128)(2,1)S(1)} copy(bf16[64,9,64]{2,0,1:T(8,128)(2,1)} %bitcast.43) | data formatting | bytes 147456 | tf_op jit(solution)/shard_map/transpose | solution.py:464
  1.7 0.0 copy-start.3
  1.7 0.1 copy.38.wf
  1.8 0.8 %copy-done.3 = bf16[9,64,64]{2,1,0:T(8,128)(2,1)S(1)} copy-done((bf16[9,64,64]{2,1,0:T(8,128)(2,1)S(1)}, bf16[9,64,64]{2,1,0:T(8,128)(2,1)}, u32[]{:S(2)}) %copy-start.3) | copy-done | bytes 73752
  2.6 0.0 copy-start.2
  2.6 0.1 copy.39.wb
  2.8 0.7 %copy-done.2 = bf16[7,64,64]{2,1,0:T(8,128)(2,1)S(1)} copy-done((bf16[7,64,64]{2,1,0:T(8,128)(2,1)S(1)}, bf16[7,64,64]{2,1,0:T(8,128)(2,1)}, u32[]{:S(2)}) %copy-start.2) | copy-done | bytes 57368
  3.5 0.0 copy-start
  3.5 0.0 copy-start.1
  3.6 0.1 copy.34
  3.7 0.1 copy.35
  3.8 0.1 copy.37
  3.9 0.1 copy.36
  4.0 0.1 fusion.1.bigw_t
  4.1 0.1 pad_maximum_fusion
  4.3 0.1 copy.40.bigw
  4.4 0.4 copy-done
  4.7 0.3 copy-done.1
  5.1 2.5 %copy_bitcast_fusion = (bf16[8,2,64,512]{3,2,1,0:T(8,128)(2,1)}, bf16[8,2,64,512]{3,2,1,0:T(8,128)(2,1)}) fusion(bf16[64,2,8,512]{3,2,1,0:T(8,128)(2,1)S(1)} %copy-done, bf16[64,2,8,512]{3,2,1,0:T(8,128)(2,1)S(1)} %copy-done.1), kind=kLoop, calls=%fused_computation | loop fusion | bytes 4194304 | tf_op jit(solution)/shard_map/transpose | solution.py:463
  7.5 62.3 %shard_map.67 = (bf16[8,2,64,512]{3,2,1,0:T(8,128)(2,1)S(1)}, f32[8,12,8,128]{3,2,1,0:T(8,128)S(1)}) custom-call(bf16[8,2,64,512]{3,2,1,0:T(8,128)(2,1)} %get-tuple-element.23.vol, bf16[8,2,64,512]{3,2,1,0:T(8,128)(2,1)} %get-tuple-element.22.og, bf16[64,576]{1,0:T(8,128)(2,1)S(1)} %copy.38.wf, bf16[64,576]{1,0:T(8,128)(2,1)S(1)} %copy.39.wb, ...), custom_call_target="tpu_custom_call" | custom-call | tf_op jit(solution)/shard_map/pallas_call | solution.py:477
  69.8 1.5 %copy.45 = bf16[64,2,8,512]{3,2,1,0:T(8,128)(2,1)} copy(bf16[64,2,8,512]{3,0,1,2:T(8,128)(2,1)S(1)} %bitcast.37) | data formatting | bytes 2097152
  71.5 0.2 reshape.44
  71.8 0.7 slice.34
  72.5 0.5 reshape.47
  73.0 0.3 fusion
  73.3 0.7 pad_add_fusion
  (7 shorter events, 0.2 us)
Async XLA Ops:
  1.7 0.9 %copy-start.3 = (bf16[9,64,64]{2,1,0:T(8,128)(2,1)S(1)}, bf16[9,64,64]{2,1,0:T(8,128)(2,1)}, u32[]{:S(2)}) copy-start(bf16[9,64,64]{2,1,0:T(8,128)(2,1)} %param.6) | copy-start | bytes 221188
  2.6 0.9 %copy-start.2 = (bf16[7,64,64]{2,1,0:T(8,128)(2,1)S(1)}, bf16[7,64,64]{2,1,0:T(8,128)(2,1)}, u32[]{:S(2)}) copy-start(bf16[7,64,64]{2,1,0:T(8,128)(2,1)} %param.7) | copy-start | bytes 172036
  3.5 1.2 %copy-start = (bf16[64,2,8,512]{3,2,1,0:T(8,128)(2,1)S(1)}, bf16[64,2,8,512]{3,2,1,0:T(8,128)(2,1)}, u32[]{:S(2)}) copy-start(bf16[64,2,8,512]{3,2,1,0:T(8,128)(2,1)} %param.5) | copy-start | bytes 3145732
  3.5 1.5 %copy-start.1 = (bf16[64,2,8,512]{3,2,1,0:T(8,128)(2,1)S(1)}, bf16[64,2,8,512]{3,2,1,0:T(8,128)(2,1)}, u32[]{:S(2)}) copy-start(bf16[64,2,8,512]{3,2,1,0:T(8,128)(2,1)} %param.4) | copy-start | bytes 3145732

commit v2 on v1

--- a/solution.py
+++ b/solution.py
@@ -120,7 +120,9 @@
 BF16 = jnp.bfloat16
 F32 = jnp.float32
 MESH = pl.DeviceIdType.MESH
-TILES = 12
+DEPTH_ROWS = 32
+PLANE_ROWS = 48
+ALL_ROWS = 80
 
 
 def sigmoid_of(values):
@@ -146,11 +148,12 @@
 
 def block_kernel(
     n, m, rows, scale,
-    vol, og, wf, wb, bigw, bigw_t,
-    vg, gsum,
+    vol, og, plane_w, depth_w,
+    vg, plane_out, depth_out,
+    wf, wb, bigw, bigw_t,
     volh, stack, slope, acts_out, acts_in, og_in, dg, ag_out, ag_in, pg_halo, plane_acc, depth_acc,
-    red_src, red_in, part, part_in, tot, tot_in,
-    vh_s, vh_r, og_s, og_r, ac_s, ac_r, ag_s, ag_r, ph_s, ph_r, r1_s, r1_r, r2_s, r2_r, r3_s, r3_r,
+    red_f, zr_src, zr_in, red_src, red_in, part, part_in, tot, tot_in,
+    vh_s, vh_r, og_s, og_r, ac_s, ac_r, ag_s, ag_r, ph_s, ph_r, z1_s, z1_r, r1_s, r1_r, r2_s, r2_r, r3_s, r3_r,
 ):
     me = lax.axis_index("wide")
     mine = lax.axis_index("narrow")
@@ -179,6 +182,17 @@
     def _(step):
         pl.semaphore_signal(barrier, inc=1, device_id={"narrow": narrow_peer(step)}, device_id_type=MESH)
 
+    for t in range(4):
+        wf[:, 128 * t : 128 * (t + 1)] = jnp.concatenate([plane_w[2 * t], plane_w[2 * t + 1]], axis=1)
+        pair = jnp.concatenate([plane_w[8 - 2 * t], plane_w[7 - 2 * t]], axis=0)
+        wb[:, 128 * t : 128 * (t + 1)] = pair.astype(F32).T.astype(BF16)
+    wf[:, 512:576] = plane_w[8]
+    wb[:, 512:576] = plane_w[0].astype(F32).T.astype(BF16)
+    for q in range(4):
+        band = jnp.concatenate([depth_w[3 - q + p] for p in range(4)], axis=1)
+        bigw[q * ch : (q + 1) * ch] = band
+        bigw_t[:, q * ch : (q + 1) * ch] = band.astype(F32).T.astype(BF16)
+
     pl.semaphore_wait(barrier, n + m - 2)
 
     has_low = mine > 0
@@ -217,6 +231,12 @@
 
     def pg_down():
         return rcopy(stack.at[1, :, pl.ds(ch, ch)], pg_halo.at[1], ph_s.at[1], ph_r.at[1], narrow=down)
+
+    def z1_copy(peer):
+        return rcopy(zr_src.at[peer], zr_in.at[me], z1_s.at[peer], z1_r.at[me], wide=peer)
+
+    def z1_arrival(peer):
+        return rcopy(zr_src.at[peer], zr_in.at[peer], z1_s.at[peer], z1_r.at[peer], wide=peer)
 
     def r1_copy(peer):
         return rcopy(red_src.at[peer], red_in.at[me], r1_s.at[peer], r1_r.at[me], wide=peer)
@@ -329,13 +349,26 @@
         for b in range(2):
             depth_acc[...] += dot_nt(dg[half, b], acts_in[:, half, b].reshape(4 * ch, cols))
 
-    for d in range(-3, 3):
+    def diagonal(d):
         tile = jnp.zeros((ch, 128), F32)
         for q in range(4):
             for t in range(2):
                 if 2 * t - q == d:
                     tile = tile + depth_acc[q * ch : (q + 1) * ch, 128 * t : 128 * (t + 1)]
-        red_src[:, d + 3] = tile.reshape(n, ch // n, 128)
+        return tile
+
+    in_low = lax.broadcasted_iota(jnp.int32, (ch, 128), 1) < ch
+    for t in range(4):
+        crossed = jnp.where(in_low, diagonal(2 * t - 2), diagonal(2 * t - 4))
+        tile = diagonal(2 * t - 3) + pltpu.roll(crossed, 64, 1)
+        red_f[:, 8 * t : 8 * (t + 1)] = tile.reshape(n, ch // n, 128)
+    zr_src[...] = red_f[:, 0:DEPTH_ROWS].astype(BF16)
+
+    @pl.loop(1, n)
+    def _(step):
+        z1_copy(wide_peer(step)).start()
+
+    zr_in[me] = zr_src[me]
 
     @pl.loop(0, rows)
     def _(step):
@@ -362,11 +395,14 @@
                 pg_down().start()
 
     for s in range(3):
-        red_src[:, 6 + 2 * s] = plane_acc[s * ch : (s + 1) * ch, 0:128].reshape(n, ch // n, 128)
+        first = plane_acc[s * ch : (s + 1) * ch, 0:128]
         rest = jnp.concatenate(
             [plane_acc[s * ch : (s + 1) * ch, 128:192], jnp.zeros((ch, 64), F32)], axis=1
         )
-        red_src[:, 7 + 2 * s] = rest.reshape(n, ch // n, 128)
+        low = DEPTH_ROWS + 16 * s
+        red_f[:, low : low + 8] = first.reshape(n, ch // n, 128)
+        red_f[:, low + 8 : low + 16] = rest.reshape(n, ch // n, 128)
+    red_src[...] = red_f[:, DEPTH_ROWS:ALL_ROWS].astype(BF16)
 
     @pl.loop(1, n)
     def _(step):
@@ -385,9 +421,11 @@
 
     @pl.loop(1, n)
     def _(step):
+        z1_arrival(wide_peer(step)).wait_recv()
         r1_arrival(wide_peer(step)).wait_recv()
 
-    part[...] = jnp.sum(red_in[...], axis=0)
+    part[0:DEPTH_ROWS] = jnp.sum(zr_in[...].astype(F32), axis=0).astype(BF16)
+    part[DEPTH_ROWS:ALL_ROWS] = jnp.sum(red_in[...].astype(F32), axis=0).astype(BF16)
 
     @pl.loop(1, m)
     def _(step):
@@ -400,7 +438,7 @@
     def _(step):
         r2_arrival(narrow_peer(step)).wait_recv()
 
-    tot[...] = jnp.sum(part_in[...], axis=0) * scale
+    tot[...] = (jnp.sum(part_in[...].astype(F32), axis=0) * scale).astype(BF16)
 
     @pl.loop(1, n)
     def _(step):
@@ -447,6 +485,7 @@
         og_copy(step).wait_send()
         act_copy(peer).wait_send()
         ag_copy(peer).wait_send()
+        z1_copy(peer).wait_send()
         r1_copy(peer).wait_send()
         r3_copy(peer).wait_send()
 
@@ -454,32 +493,45 @@
     def _(step):
         r2_copy(narrow_peer(step)).wait_send()
 
-    gsum[...] = tot_in[...]
+    red_f[...] = tot_in[...].astype(F32)
+    for t in range(4):
+        tile = red_f[:, 8 * t : 8 * (t + 1)].reshape(ch, 128)
+        depth_out[2 * t] = tile[:, 0:64]
+        if t < 3:
+            depth_out[2 * t + 1] = tile[:, 64:128]
+    for s in range(3):
+        low = DEPTH_ROWS + 16 * s
+        first = red_f[:, low : low + 8].reshape(ch, 128)
+        plane_out[2 - s] = first[:, 0:64]
+        plane_out[5 - s] = first[:, 64:128]
+        plane_out[8 - s] = red_f[:, low + 8 : low + 16].reshape(ch, 128)[:, 0:64]
 
 
 def fused_block(n, m, volume, out_grad, plane_kernel, z_axis_kernel):
     ch, _, rows, cols = volume.shape
     vol = volume.transpose(2, 1, 0, 3)
     og = out_grad.transpose(2, 1, 0, 3)
-    wf = plane_kernel.transpose(1, 0, 2).reshape(ch, 9 * ch)
-    wb = plane_kernel[::-1].transpose(2, 0, 1).reshape(ch, 9 * ch)
-    bigw = jnp.concatenate(
-        [z_axis_kernel[3 - q : 7 - q].transpose(1, 0, 2).reshape(ch, 4 * ch) for q in range(4)], axis=0
-    )
     scale = 1.0 / math.sqrt(2 * n * rows * m * cols)
     own = (rows, 2, ch, cols)
     pencil = (4, 2, 2, ch, cols)
-    piece = (TILES, ch // n, 128)
     sems = []
-    for count in (2, n, n, n, 2, n, m, n):
+    for count in (2, n, n, n, 2, n, n, m, n):
         sems += [pltpu.SemaphoreType.DMA((count,))] * 2
     vmem = pl.BlockSpec(memory_space=pltpu.VMEM)
-    vg, gsum = pl.pallas_call(
+    vg, plane, depth = pl.pallas_call(
         functools.partial(block_kernel, n, m, rows, scale),
-        out_shape=(jax.ShapeDtypeStruct(own, BF16), jax.ShapeDtypeStruct((n,) + piece, F32)),
-        in_specs=[vmem] * 6,
-        out_specs=(vmem, vmem),
+        out_shape=(
+            jax.ShapeDtypeStruct(own, BF16),
+            jax.ShapeDtypeStruct((9, ch, ch), F32),
+            jax.ShapeDtypeStruct((7, ch, ch), F32),
+        ),
+        in_specs=[vmem] * 4,
+        out_specs=(vmem, vmem, vmem),
         scratch_shapes=[
+            pltpu.VMEM((ch, 9 * ch), BF16),
+            pltpu.VMEM((ch, 9 * ch), BF16),
+            pltpu.VMEM((4 * ch, 4 * ch), BF16),
+            pltpu.VMEM((4 * ch, 4 * ch), BF16),
             pltpu.VMEM((rows + 2, 2, ch, cols), BF16),
             pltpu.VMEM((rows + 2, 2, 3 * ch, cols), BF16),
             pltpu.VMEM(own, F32),
@@ -492,25 +544,21 @@
             pltpu.VMEM((2, 2, ch, cols), BF16),
             pltpu.VMEM((3 * ch, 3 * ch), F32),
             pltpu.VMEM((4 * ch, 4 * ch), F32),
-            pltpu.VMEM((n,) + piece, F32),
-            pltpu.VMEM((n,) + piece, F32),
-            pltpu.VMEM(piece, F32),
-            pltpu.VMEM((m,) + piece, F32),
-            pltpu.VMEM(piece, F32),
-            pltpu.VMEM((n,) + piece, F32),
+            pltpu.VMEM((n, ALL_ROWS, 128), F32),
+            pltpu.VMEM((n, DEPTH_ROWS, 128), BF16),
+            pltpu.VMEM((n, DEPTH_ROWS, 128), BF16),
+            pltpu.VMEM((n, PLANE_ROWS, 128), BF16),
+            pltpu.VMEM((n, PLANE_ROWS, 128), BF16),
+            pltpu.VMEM((ALL_ROWS, 128), BF16),
+            pltpu.VMEM((m, ALL_ROWS, 128), BF16),
+            pltpu.VMEM((ALL_ROWS, 128), BF16),
+            pltpu.VMEM((n, ALL_ROWS, 128), BF16),
         ]
         + sems,
         compiler_params=pltpu.CompilerParams(
             collective_id=0, has_side_effects=True, vmem_limit_bytes=52 * 1024 * 1024
         ),
-    )(vol, og, wf, wb, bigw, bigw.T)
-    tiles = gsum.transpose(1, 0, 2, 3).reshape(TILES, ch, 2, ch)
-    low = tiles[:6, :, 0]
-    high = tiles[:6, :, 1]
-    edge = jnp.zeros((1, ch, ch), F32)
-    depth = jnp.concatenate([low, edge]) + jnp.concatenate([edge, high])
-    plane = tiles[6:].reshape(3, 2, ch, 2, ch)[::-1].transpose(1, 3, 0, 2, 4)
-    plane = plane.reshape(4, 3, ch, ch)[:3].reshape(9, ch, ch)
+    )(vol, og, plane_kernel, z_axis_kernel)
     return vg.transpose(2, 1, 0, 3), plane, depth
 
 

time: 74.3 us -> 66.8 us (0.90)
  Pallas kernels: 62.3 us -> 58.9 us
  local copies, waits for them, and re-layouts: 10 us -> 7.01 us
  other arithmetic: 0.97 us -> 0 us
    pallas_call x1, Pallas kernels: 62.3 us -> 58.9 us  [fused_block(): pl.pallas_call(functools.partial(block_kernel, n, m, rows, scale), out_sh...]
    transpose x9 -> x0, local copies, waits for them, and re-layouts: 1.59 us -> none  [the longest x1 1.05 us: fused_block(): wf = plane_kernel.transpose(1, 0, 2).reshape(ch, 9 * ch)]
    transpose x1, local copies, waits for them, and re-layouts: 2.47 us -> 4.05 us  [fused_block(): og = out_grad.transpose(2, 1, 0, 3)]
    slice x4 -> x0, local copies, waits for them, and re-layouts: 1.1 us -> none  [the longest x1 0.74 us: fused_block(): plane = plane.reshape(4, 3, ch, ch)[:3].reshape(9, ch, ch)]
    reshape x4 -> x0, local copies, waits for them, and re-layouts: 0.99 us -> none  [the longest x1 0.46 us: fused_block(): tiles = gsum.transpose(1, 0, 2, 3).reshape(TILES, ch, 2, ch)]
    unnamed x9 -> x7, local copies, waits for them, and re-layouts: 3.76 us -> 2.96 us
where the time goes in v2:
time: 66.8 us; the launch traced here: 66.6 us
  Pallas kernels  58.9 us (88%)
  local copies, waits for them, and re-layouts  7.01 us (10%)
    pallas_call x1, Pallas kernels, fused_block(): pl.pallas_call(functools.partial(block_kernel, n, m, rows, scale), out_sh...  58.9 us
    transpose x1, local copies, waits for them, and re-layouts, fused_block(): og = out_grad.transpose(2, 1, 0, 3)  4.05 us
    unnamed x7, local copies, waits for them, and re-layouts  2.96 us

profile of v2, /device:TPU:0, one launch (start us, length us, event | category | flops | bytes accessed | tf_op | source)
XLA Modules:
  0.0 66.6 jit_solution(1816967461785634636)
XLA Ops:
  0.6 0.0 copy-start.1
  0.6 0.0 copy-start
  0.7 4.1 %copy_bitcast_fusion = (bf16[8,2,64,512]{3,2,1,0:T(8,128)(2,1)}, bf16[8,2,64,512]{3,2,1,0:T(8,128)(2,1)}) fusion(bf16[64,2,8,512]{3,2,1,0:T(8,128)(2,1)} %param.5, bf16[64,2,8,512]{3,2,1,0:T(8,128)(2,1)} %param.4), kind=kLoop, calls=%fused_computation | loop fusion | bytes 4194304 | tf_op jit(solution)/shard_map/transpose | solution.py:513
  4.7 0.0 copy-done.1
  4.7 0.0 copy-done
  4.7 58.9 %shard_map.67 = (bf16[8,2,64,512]{3,2,1,0:T(8,128)(2,1)S(1)}, f32[9,64,64]{2,1,0:T(8,128)S(1)}, f32[7,64,64]{2,1,0:T(8,128)S(1)}) custom-call(bf16[8,2,64,512]{3,2,1,0:T(8,128)(2,1)} %get-tuple-element.13.vol, bf16[8,2,64,512]{3,2,1,0:T(8,128)(2,1)} %get-tuple-element.12.og, bf16[9,64,64]{2,1,0:T(8,128)(2,1)S(1)} %copy-done, bf16[7,64,64]{2,1,0:T(8,128)(2,1)S(1)} %copy-done.1), custom_call_target="tpu_custom_call" | custom-call | tf_op jit(solution)/shard_map/pallas_call | solution.py:521
  63.7 1.5 %copy.9 = bf16[64,2,8,512]{3,2,1,0:T(8,128)(2,1)} copy(bf16[64,2,8,512]{3,0,1,2:T(8,128)(2,1)S(1)} %bitcast.5) | data formatting | bytes 2097152
  65.2 0.7 %copy.14 = f32[9,64,64]{2,1,0:T(8,128)} copy(f32[9,64,64]{2,1,0:T(8,128)S(1)} %get-tuple-element.18) | data formatting | bytes 294912
  65.9 0.7 %copy.15 = f32[7,64,64]{2,1,0:T(8,128)} copy(f32[7,64,64]{2,1,0:T(8,128)S(1)} %get-tuple-element.19) | data formatting | bytes 229376
Async XLA Ops:
  0.6 4.1 %copy-start.1 = (bf16[7,64,64]{2,1,0:T(8,128)(2,1)S(1)}, bf16[7,64,64]{2,1,0:T(8,128)(2,1)}, u32[]{:S(2)}) copy-start(bf16[7,64,64]{2,1,0:T(8,128)(2,1)} %depth_w.1) | copy-start | bytes 172036
  0.6 4.1 %copy-start = (bf16[9,64,64]{2,1,0:T(8,128)(2,1)S(1)}, bf16[9,64,64]{2,1,0:T(8,128)(2,1)}, u32[]{:S(2)}) copy-start(bf16[9,64,64]{2,1,0:T(8,128)(2,1)} %plane_w.1) | copy-start | bytes 221188

commit v3 on v2

--- a/solution.py
+++ b/solution.py
@@ -206,31 +206,51 @@
     def vol_down():
         return rcopy(vol.at[0], volh.at[rows + 1], vh_s.at[1], vh_r.at[1], narrow=down)
 
-    def og_copy(step):
-        peer = wide_peer(step)
-        return rcopy(og.at[peer], og_in.at[me // 2, lax.rem(me, 2)], og_s.at[peer], og_r.at[me], wide=peer)
-
-    def og_arrival(step):
-        peer = wide_peer(step)
-        return rcopy(og.at[peer], og_in.at[peer // 2, lax.rem(peer, 2)], og_s.at[peer], og_r.at[peer], wide=peer)
-
-    def act_copy(peer):
-        return rcopy(acts_out.at[peer], acts_in.at[me // 2, lax.rem(me, 2)], ac_s.at[peer], ac_r.at[me], wide=peer)
-
-    def act_arrival(peer):
-        return rcopy(acts_out.at[peer], acts_in.at[peer // 2, lax.rem(peer, 2)], ac_s.at[peer], ac_r.at[peer], wide=peer)
-
-    def ag_copy(peer):
-        return rcopy(ag_out.at[peer // 2, lax.rem(peer, 2)], ag_in.at[me], ag_s.at[peer], ag_r.at[me], wide=peer)
-
-    def ag_arrival(peer):
-        return rcopy(ag_out.at[peer // 2, lax.rem(peer, 2)], ag_in.at[peer], ag_s.at[peer], ag_r.at[peer], wide=peer)
-
-    def pg_up():
-        return rcopy(stack.at[rows, :, pl.ds(ch, ch)], pg_halo.at[0], ph_s.at[0], ph_r.at[0], narrow=up)
-
-    def pg_down():
-        return rcopy(stack.at[1, :, pl.ds(ch, ch)], pg_halo.at[1], ph_s.at[1], ph_r.at[1], narrow=down)
+    def og_copy(peer, z):
+        return rcopy(
+            og.at[peer, z], og_in.at[me // 2, lax.rem(me, 2), z],
+            og_s.at[n * z + peer], og_r.at[n * z + me], wide=peer,
+        )
+
+    def og_arrival(peer, z):
+        return rcopy(
+            og.at[peer, z], og_in.at[peer // 2, lax.rem(peer, 2), z],
+            og_s.at[n * z + peer], og_r.at[n * z + peer], wide=peer,
+        )
+
+    def act_copy(peer, z):
+        return rcopy(
+            acts_out.at[peer, z], acts_in.at[me // 2, lax.rem(me, 2), z],
+            ac_s.at[n * z + peer], ac_r.at[n * z + me], wide=peer,
+        )
+
+    def act_arrival(peer, z):
+        return rcopy(
+            acts_out.at[peer, z], acts_in.at[peer // 2, lax.rem(peer, 2), z],
+            ac_s.at[n * z + peer], ac_r.at[n * z + peer], wide=peer,
+        )
+
+    def ag_copy(peer, z):
+        return rcopy(
+            ag_out.at[peer // 2, lax.rem(peer, 2), z], ag_in.at[me, z],
+            ag_s.at[n * z + peer], ag_r.at[n * z + me], wide=peer,
+        )
+
+    def ag_arrival(peer, z):
+        return rcopy(
+            ag_out.at[peer // 2, lax.rem(peer, 2), z], ag_in.at[peer, z],
+            ag_s.at[n * z + peer], ag_r.at[n * z + peer], wide=peer,
+        )
+
+    def pg_up(z):
+        return rcopy(
+            stack.at[rows, z, pl.ds(ch, ch)], pg_halo.at[0, z], ph_s.at[2 * z], ph_r.at[2 * z], narrow=up
+        )
+
+    def pg_down(z):
+        return rcopy(
+            stack.at[1, z, pl.ds(ch, ch)], pg_halo.at[1, z], ph_s.at[2 * z + 1], ph_r.at[2 * z + 1], narrow=down
+        )
 
     def z1_copy(peer):
         return rcopy(zr_src.at[peer], zr_in.at[me], z1_s.at[peer], z1_r.at[me], wide=peer)
@@ -266,7 +286,7 @@
 
     @pl.loop(1, n)
     def _(step):
-        og_copy(step).start()
+        og_copy(wide_peer(step), 0).start()
 
     og_in[me // 2, lax.rem(me, 2)] = og[me]
 
@@ -278,12 +298,32 @@
     def _():
         volh[rows + 1] = jnp.zeros(volh.shape[1:], BF16)
 
-    @pl.loop(0, rows)
-    def _(x):
-        for z in range(2):
+    def stack_rows(z):
+        @pl.loop(0, rows)
+        def _(x):
             row = vol[x, z]
             volh[x + 1, z] = row
             stack[x + 1, z] = shifted_stack(row)
+
+    def forward_rows(z):
+        for x in (0, rows + 1):
+            stack[x, z] = shifted_stack(volh[x, z])
+
+        @pl.loop(1, n + 1)
+        def _(step):
+            x = wide_peer(step)
+            v = dot_nn(wf[...], stack[pl.ds(x, 3), z].reshape(9 * ch, cols))
+            g = sigmoid_of(v)
+            acts_out[x, z] = (v * g).astype(BF16)
+            slope[x, z] = g * (1.0 + v * (1.0 - g))
+
+            @pl.when(step < n)
+            def _():
+                act_copy(x, z).start()
+
+        acts_in[me // 2, lax.rem(me, 2), z] = acts_out[me, z]
+
+    stack_rows(0)
 
     @pl.when(has_high)
     def _():
@@ -295,59 +335,47 @@
         vol_down().wait_send()
         vol_up().wait_recv()
 
-    for x in (0, rows + 1):
-        for z in range(2):
-            stack[x, z] = shifted_stack(volh[x, z])
-
-    @pl.loop(1, n + 1)
-    def _(step):
-        x = wide_peer(step)
-        for z in range(2):
-            v = dot_nn(wf[...], stack[pl.ds(x, 3), z].reshape(9 * ch, cols))
-            g = sigmoid_of(v)
-            acts_out[x, z] = (v * g).astype(BF16)
-            slope[x, z] = g * (1.0 + v * (1.0 - g))
-
-        @pl.when(step < n)
-        def _():
-            act_copy(x).start()
-
-    acts_in[me // 2, lax.rem(me, 2)] = acts_out[me]
-
-    @pl.loop(1, n)
-    def _(step):
-        og_arrival(step).wait_recv()
-        act_arrival(wide_peer(step)).wait_recv()
-
-    @pl.loop(0, 2)
-    def _(half):
-        for b in range(2):
-            pencil = acts_in[:, half, b].reshape(4 * ch, cols)
+    forward_rows(0)
+
+    @pl.loop(1, n)
+    def _(step):
+        og_copy(wide_peer(step), 1).start()
+
+    stack_rows(1)
+    forward_rows(1)
+    depth_acc[...] = jnp.zeros_like(depth_acc)
+    plane_acc[...] = jnp.zeros_like(plane_acc)
+
+    for z in range(2):
+        @pl.loop(1, n)
+        def _(step):
+            og_arrival(wide_peer(step), z).wait_recv()
+            act_arrival(wide_peer(step), z).wait_recv()
+
+        @pl.loop(0, 2)
+        def _(half):
+            pencil = acts_in[:, half, z].reshape(4 * ch, cols)
             v = dot_nn(bigw[...], pencil)
             g = sigmoid_of(v)
-            cot = og_in[:, half, b].reshape(4 * ch, cols).astype(F32)
+            cot = og_in[:, half, z].reshape(4 * ch, cols).astype(F32)
             grad = (cot * (g * (1.0 + v * (1.0 - g)))).astype(BF16)
-            dg[half, b] = grad
+            dg[half, z] = grad
             back = dot_nn(bigw_t[...], grad).astype(BF16)
-            ag_out[:, half, b] = back.reshape(4, ch, cols)
-        for q in range(4):
-            peer = 2 * q + half
-
-            @pl.when(peer != me)
-            def _():
-                ag_copy(peer).start()
-
-            @pl.when(peer == me)
-            def _():
-                ag_in[me] = ag_out[q, half]
-
-    depth_acc[...] = jnp.zeros_like(depth_acc)
-    plane_acc[...] = jnp.zeros_like(plane_acc)
-
-    @pl.loop(0, 2)
-    def _(half):
-        for b in range(2):
-            depth_acc[...] += dot_nt(dg[half, b], acts_in[:, half, b].reshape(4 * ch, cols))
+            ag_out[:, half, z] = back.reshape(4, ch, cols)
+            for q in range(4):
+                peer = 2 * q + half
+
+                @pl.when(peer != me)
+                def _():
+                    ag_copy(peer, z).start()
+
+                @pl.when(peer == me)
+                def _():
+                    ag_in[me, z] = ag_out[q, half, z]
+
+        @pl.loop(0, 2)
+        def _(half):
+            depth_acc[...] += dot_nt(dg[half, z], acts_in[:, half, z].reshape(4 * ch, cols))
 
     def diagonal(d):
         tile = jnp.zeros((ch, 128), F32)
@@ -370,29 +398,63 @@
 
     zr_in[me] = zr_src[me]
 
-    @pl.loop(0, rows)
-    def _(step):
-        x = lax.rem(step + rows - 1, rows)
-
-        @pl.when(x != me)
-        def _():
-            ag_arrival(x).wait_recv()
-
-        for z in range(2):
+    def pre_rows(z):
+        @pl.loop(0, rows)
+        def _(step):
+            x = lax.rem(step + rows - 1, rows)
+
+            @pl.when(x != me)
+            def _():
+                ag_arrival(x, z).wait_recv()
+
             row = ag_in[x, z].astype(F32) * slope[x, z]
             shifted = shifted_stack(row.astype(BF16))
             stack[x + 1, z] = shifted
             plane_acc[...] += dot_nt(shifted, volh[pl.ds(x, 3), z].reshape(3 * ch, cols))
 
-        @pl.when(step == 1)
+            @pl.when(step == 1)
+            def _():
+                @pl.when(has_high)
+                def _():
+                    pg_up(z).start()
+
+                @pl.when(has_low)
+                def _():
+                    pg_down(z).start()
+
+    def volume_rows(z, low, high):
+        @pl.loop(low, high)
+        def _(x):
+            out = dot_nn(wb[...], stack[pl.ds(x, 3), z].reshape(9 * ch, cols))
+            vg[x, z] = (og[x, z].astype(F32) + out).astype(BF16)
+
+    def edge_rows(z):
+        @pl.when(has_high)
         def _():
-            @pl.when(has_high)
-            def _():
-                pg_up().start()
-
-            @pl.when(has_low)
-            def _():
-                pg_down().start()
+            pg_up(z).wait_send()
+            pg_down(z).wait_recv()
+            stack[rows + 1, z] = shifted_stack(pg_halo[1, z])
+
+        @pl.when(has_low)
+        def _():
+            pg_down(z).wait_send()
+            pg_up(z).wait_recv()
+            stack[0, z] = shifted_stack(pg_halo[0, z])
+
+        @pl.when(jnp.logical_not(has_low))
+        def _():
+            stack[0, z] = jnp.zeros(stack.shape[2:], BF16)
+
+        @pl.when(jnp.logical_not(has_high))
+        def _():
+            stack[rows + 1, z] = jnp.zeros(stack.shape[2:], BF16)
+
+        volume_rows(z, 0, 1)
+        volume_rows(z, rows - 1, rows)
+
+    pre_rows(0)
+    volume_rows(0, 1, rows - 1)
+    pre_rows(1)
 
     for s in range(3):
         first = plane_acc[s * ch : (s + 1) * ch, 0:128]
@@ -410,14 +472,7 @@
 
     red_in[me] = red_src[me]
 
-    def volume_rows(low, high):
-        @pl.loop(low, high)
-        def _(x):
-            for z in range(2):
-                out = dot_nn(wb[...], stack[pl.ds(x, 3), z].reshape(9 * ch, cols))
-                vg[x, z] = (og[x, z].astype(F32) + out).astype(BF16)
-
-    volume_rows(1, 3)
+    volume_rows(1, 1, 4)
 
     @pl.loop(1, n)
     def _(step):
@@ -432,7 +487,7 @@
         r2_copy(narrow_peer(step)).start()
 
     part_in[mine] = part[...]
-    volume_rows(3, 5)
+    edge_rows(0)
 
     @pl.loop(1, m)
     def _(step):
@@ -445,46 +500,17 @@
         r3_copy(wide_peer(step)).start()
 
     tot_in[me] = tot[...]
-    volume_rows(5, rows - 1)
-
-    @pl.when(has_high)
-    def _():
-        pg_up().wait_send()
-        pg_down().wait_recv()
-
-    @pl.when(has_low)
-    def _():
-        pg_down().wait_send()
-        pg_up().wait_recv()
-
-    @pl.when(has_low)
-    def _():
-        for z in range(2):
-            stack[0, z] = shifted_stack(pg_halo[0, z])
-
-    @pl.when(has_high)
-    def _():
-        for z in range(2):
-            stack[rows + 1, z] = shifted_stack(pg_halo[1, z])
-
-    @pl.when(jnp.logical_not(has_low))
-    def _():
-        stack[0] = jnp.zeros(stack.shape[1:], BF16)
-
-    @pl.when(jnp.logical_not(has_high))
-    def _():
-        stack[rows + 1] = jnp.zeros(stack.shape[1:], BF16)
-
-    volume_rows(0, 1)
-    volume_rows(rows - 1, rows)
+    volume_rows(1, 4, rows - 1)
+    edge_rows(1)
 
     @pl.loop(1, n)
     def _(step):
         peer = wide_peer(step)
         r3_arrival(peer).wait_recv()
-        og_copy(step).wait_send()
-        act_copy(peer).wait_send()
-        ag_copy(peer).wait_send()
+        for z in range(2):
+            og_copy(peer, z).wait_send()
+            act_copy(peer, z).wait_send()
+            ag_copy(peer, z).wait_send()
         z1_copy(peer).wait_send()
         r1_copy(peer).wait_send()
         r3_copy(peer).wait_send()
@@ -515,7 +541,7 @@
     own = (rows, 2, ch, cols)
     pencil = (4, 2, 2, ch, cols)
     sems = []
-    for count in (2, n, n, n, 2, n, n, m, n):
+    for count in (2, 2 * n, 2 * n, 2 * n, 4, n, n, m, n):
         sems += [pltpu.SemaphoreType.DMA((count,))] * 2
     vmem = pl.BlockSpec(memory_space=pltpu.VMEM)
     vg, plane, depth = pl.pallas_call(

time: 66.8 us -> 64.2 us (0.961)
  Pallas kernels: 58.9 us -> 56.3 us
    pallas_call x1, Pallas kernels: 58.9 us -> 56.3 us  [fused_block(): pl.pallas_call(functools.partial(block_kernel, n, m, rows, scale), out_sh...]
where the time goes in v3:
time: 64.2 us; the launch traced here: 64 us
  Pallas kernels  56.3 us (88%)
  local copies, waits for them, and re-layouts  7.01 us (11%)
  between operations  0.66 us (1%)
    pallas_call x1, Pallas kernels, fused_block(): pl.pallas_call(functools.partial(block_kernel, n, m, rows, scale), out_sh...  56.3 us
    transpose x1, local copies, waits for them, and re-layouts, fused_block(): og = out_grad.transpose(2, 1, 0, 3)  4.05 us
    unnamed x7, local copies, waits for them, and re-layouts  2.96 us

profile of v3, /device:TPU:0, one launch (start us, length us, event | category | flops | bytes accessed | tf_op | source)
XLA Modules:
  0.0 64.0 jit_solution(14625276687657913450)
XLA Ops:
  0.6 0.0 copy-start.1
  0.6 0.0 copy-start
  0.7 4.1 %copy_bitcast_fusion = (bf16[8,2,64,512]{3,2,1,0:T(8,128)(2,1)}, bf16[8,2,64,512]{3,2,1,0:T(8,128)(2,1)}) fusion(bf16[64,2,8,512]{3,2,1,0:T(8,128)(2,1)} %param.5, bf16[64,2,8,512]{3,2,1,0:T(8,128)(2,1)} %param.4), kind=kLoop, calls=%fused_computation | loop fusion | bytes 4194304 | tf_op jit(solution)/shard_map/transpose | solution.py:539
  4.7 0.0 copy-done.1
  4.7 0.0 copy-done
  4.7 56.3 %shard_map.67 = (bf16[8,2,64,512]{3,2,1,0:T(8,128)(2,1)S(1)}, f32[9,64,64]{2,1,0:T(8,128)S(1)}, f32[7,64,64]{2,1,0:T(8,128)S(1)}) custom-call(bf16[8,2,64,512]{3,2,1,0:T(8,128)(2,1)} %get-tuple-element.13.vol, bf16[8,2,64,512]{3,2,1,0:T(8,128)(2,1)} %get-tuple-element.12.og, bf16[9,64,64]{2,1,0:T(8,128)(2,1)S(1)} %copy-done, bf16[7,64,64]{2,1,0:T(8,128)(2,1)S(1)} %copy-done.1), custom_call_target="tpu_custom_call" | custom-call | tf_op jit(solution)/shard_map/pallas_call | solution.py:547
  61.0 1.5 %copy.9 = bf16[64,2,8,512]{3,2,1,0:T(8,128)(2,1)} copy(bf16[64,2,8,512]{3,0,1,2:T(8,128)(2,1)S(1)} %bitcast.5) | data formatting | bytes 2097152
  62.6 0.7 %copy.14 = f32[9,64,64]{2,1,0:T(8,128)} copy(f32[9,64,64]{2,1,0:T(8,128)S(1)} %get-tuple-element.18) | data formatting | bytes 294912
  63.3 0.7 %copy.15 = f32[7,64,64]{2,1,0:T(8,128)} copy(f32[7,64,64]{2,1,0:T(8,128)S(1)} %get-tuple-element.19) | data formatting | bytes 229376
Async XLA Ops:
  0.6 4.1 %copy-start.1 = (bf16[7,64,64]{2,1,0:T(8,128)(2,1)S(1)}, bf16[7,64,64]{2,1,0:T(8,128)(2,1)}, u32[]{:S(2)}) copy-start(bf16[7,64,64]{2,1,0:T(8,128)(2,1)} %depth_w.1) | copy-start | bytes 172036
  0.6 4.1 %copy-start = (bf16[9,64,64]{2,1,0:T(8,128)(2,1)S(1)}, bf16[9,64,64]{2,1,0:T(8,128)(2,1)}, u32[]{:S(2)}) copy-start(bf16[9,64,64]{2,1,0:T(8,128)(2,1)} %plane_w.1) | copy-start | bytes 221188

commit v4 on v3

--- a/solution.py
+++ b/solution.py
@@ -149,7 +149,7 @@
 def block_kernel(
     n, m, rows, scale,
     vol, og, plane_w, depth_w,
-    vg, plane_out, depth_out,
+    vg, kernel_out,
     wf, wb, bigw, bigw_t,
     volh, stack, slope, acts_out, acts_in, og_in, dg, ag_out, ag_in, pg_halo, plane_acc, depth_acc,
     red_f, zr_src, zr_in, red_src, red_in, part, part_in, tot, tot_in,
@@ -167,7 +167,14 @@
         )
 
     def wide_peer(step):
-        return lax.rem(me + step, n)
+        spot = lax.rem(step * 3, 4)
+        first, second, third = lax.rem(spot, 2), lax.rem(spot // 2, 2), lax.rem(step // 4, 2)
+        core = lax.rem(me, 2)
+        dx = first * (1 - core) + second * core
+        dy = second * (1 - core) + first * core
+        x = lax.rem(lax.rem(me // 2, 2) + dx, 2)
+        y = lax.rem(me // 4 + dy, 2)
+        return 4 * y + 2 * x + lax.rem(core + third, 2)
 
     def narrow_peer(step):
         return lax.rem(mine + step, m)
@@ -522,15 +529,15 @@
     red_f[...] = tot_in[...].astype(F32)
     for t in range(4):
         tile = red_f[:, 8 * t : 8 * (t + 1)].reshape(ch, 128)
-        depth_out[2 * t] = tile[:, 0:64]
+        kernel_out[9 + 2 * t] = tile[:, 0:64]
         if t < 3:
-            depth_out[2 * t + 1] = tile[:, 64:128]
+            kernel_out[10 + 2 * t] = tile[:, 64:128]
     for s in range(3):
         low = DEPTH_ROWS + 16 * s
         first = red_f[:, low : low + 8].reshape(ch, 128)
-        plane_out[2 - s] = first[:, 0:64]
-        plane_out[5 - s] = first[:, 64:128]
-        plane_out[8 - s] = red_f[:, low + 8 : low + 16].reshape(ch, 128)[:, 0:64]
+        kernel_out[2 - s] = first[:, 0:64]
+        kernel_out[5 - s] = first[:, 64:128]
+        kernel_out[8 - s] = red_f[:, low + 8 : low + 16].reshape(ch, 128)[:, 0:64]
 
 
 def fused_block(n, m, volume, out_grad, plane_kernel, z_axis_kernel):
@@ -544,15 +551,14 @@
     for count in (2, 2 * n, 2 * n, 2 * n, 4, n, n, m, n):
         sems += [pltpu.SemaphoreType.DMA((count,))] * 2
     vmem = pl.BlockSpec(memory_space=pltpu.VMEM)
-    vg, plane, depth = pl.pallas_call(
+    vg, grads = pl.pallas_call(
         functools.partial(block_kernel, n, m, rows, scale),
         out_shape=(
             jax.ShapeDtypeStruct(own, BF16),
-            jax.ShapeDtypeStruct((9, ch, ch), F32),
-            jax.ShapeDtypeStruct((7, ch, ch), F32),
+            jax.ShapeDtypeStruct((16, ch, ch), F32),
         ),
         in_specs=[vmem] * 4,
-        out_specs=(vmem, vmem, vmem),
+        out_specs=(vmem, vmem),
         scratch_shapes=[
             pltpu.VMEM((ch, 9 * ch), BF16),
             pltpu.VMEM((ch, 9 * ch), BF16),
@@ -585,7 +591,7 @@
             collective_id=0, has_side_effects=True, vmem_limit_bytes=52 * 1024 * 1024
         ),
     )(vol, og, plane_kernel, z_axis_kernel)
-    return vg.transpose(2, 1, 0, 3), plane, depth
+    return vg.transpose(2, 1, 0, 3), grads[:9], grads[9:]
 
 
 def solution(mesh):

time: 64.2 us -> 64.1 us (level)
    slice x0 -> x2, local copies, waits for them, and re-layouts: none -> 1.44 us  [fused_block(): return (vg.transpose(2, 1, 0, 3), grads[:9], grads[9:])]
    unnamed x7 -> x5, local copies, waits for them, and re-layouts: 2.96 us -> 1.56 us
where the time goes in v4:
time: 64.1 us; the launch traced here: 63.9 us
  Pallas kernels  56.2 us (88%)
  local copies, waits for them, and re-layouts  7.05 us (11%)
  between operations  0.66 us (1%)
    pallas_call x1, Pallas kernels, fused_block(): pl.pallas_call(functools.partial(block_kernel, n, m, rows, scale), out_sh...  56.2 us
    transpose x1, local copies, waits for them, and re-layouts, fused_block(): og = out_grad.transpose(2, 1, 0, 3)  4.05 us
    unnamed x5, local copies, waits for them, and re-layouts  1.56 us
    slice x2, local copies, waits for them, and re-layouts, fused_block(): return (vg.transpose(2, 1, 0, 3), grads[:9], grads[9:])  1.44 us

profile of v4, /device:TPU:0, one launch (start us, length us, event | category | flops | bytes accessed | tf_op | source)
XLA Modules:
  0.0 63.9 jit_solution(14822757250756181677)
XLA Ops:
  0.6 0.0 copy-start.1
  0.6 0.0 copy-start
  0.7 4.1 %copy_bitcast_fusion = (bf16[8,2,64,512]{3,2,1,0:T(8,128)(2,1)}, bf16[8,2,64,512]{3,2,1,0:T(8,128)(2,1)}) fusion(bf16[64,2,8,512]{3,2,1,0:T(8,128)(2,1)} %param.5, bf16[64,2,8,512]{3,2,1,0:T(8,128)(2,1)} %param.4), kind=kLoop, calls=%fused_computation | loop fusion | bytes 4194304 | tf_op jit(solution)/shard_map/transpose | solution.py:546
  4.7 0.0 copy-done.1
  4.7 0.0 copy-done
  4.7 56.2 %shard_map.67 = (bf16[8,2,64,512]{3,2,1,0:T(8,128)(2,1)S(1)}, f32[16,64,64]{2,1,0:T(8,128)S(1)}) custom-call(bf16[8,2,64,512]{3,2,1,0:T(8,128)(2,1)} %get-tuple-element.11.vol, bf16[8,2,64,512]{3,2,1,0:T(8,128)(2,1)} %get-tuple-element.10.og, bf16[9,64,64]{2,1,0:T(8,128)(2,1)S(1)} %copy-done, bf16[7,64,64]{2,1,0:T(8,128)(2,1)S(1)} %copy-done.1), custom_call_target="tpu_custom_call" | custom-call | tf_op jit(solution)/shard_map/pallas_call | solution.py:554
  60.9 1.5 %copy.9 = bf16[64,2,8,512]{3,2,1,0:T(8,128)(2,1)} copy(bf16[64,2,8,512]{3,0,1,2:T(8,128)(2,1)S(1)} %bitcast.5) | data formatting | bytes 2097152
  62.5 0.7 %slice.7 = f32[7,64,64]{2,1,0:T(8,128)} slice(f32[16,64,64]{2,1,0:T(8,128)S(1)} %get-tuple-element.6), slice={[9:16], [0:64], [0:64]} | slice | bytes 229376 | tf_op jit(solution)/shard_map/slice | solution.py:594
  63.2 0.7 %slice.6 = f32[9,64,64]{2,1,0:T(8,128)} slice(f32[16,64,64]{2,1,0:T(8,128)S(1)} %get-tuple-element.6), slice={[0:9], [0:64], [0:64]} | slice | bytes 294912 | tf_op jit(solution)/shard_map/slice | solution.py:594
Async XLA Ops:
  0.6 4.1 %copy-start.1 = (bf16[7,64,64]{2,1,0:T(8,128)(2,1)S(1)}, bf16[7,64,64]{2,1,0:T(8,128)(2,1)}, u32[]{:S(2)}) copy-start(bf16[7,64,64]{2,1,0:T(8,128)(2,1)} %depth_w.1) | copy-start | bytes 172036
  0.6 4.1 %copy-start = (bf16[9,64,64]{2,1,0:T(8,128)(2,1)S(1)}, bf16[9,64,64]{2,1,0:T(8,128)(2,1)}, u32[]{:S(2)}) copy-start(bf16[9,64,64]{2,1,0:T(8,128)(2,1)} %plane_w.1) | copy-start | bytes 221188
